TPU v7x, 32 devices: a whole 2x2x4 slice. The times are simulated.
32 devices in a mesh: dp: 4 (over z), lat: 2 (over x), lon: 4 (over y, core).
Axes of the slice: x: 2, y: 2, z: 4, core: 2. Of those that a mesh axis runs over, the one named last changes fastest.
Arguments:
- initial_state: float32 [4, 128, 16, 512], P('dp', None, 'lat', 'lon'), may hold values from -6 to 6
- cotangent: float32 [4, 128, 16, 512], P('dp', None, 'lat', 'lon'), may hold values from -6 to 6
- diffusion: float32 [128], replicated, may hold values from 0.02 to 0.2
- norm_gain: float32 [128], replicated, may hold values from 0.5 to 1.5
- weight_in: bfloat16 [1024, 128], replicated, may hold values from -0.5 to 0.5
- bias_in: float32 [1024], replicated, may hold values from -3 to 3
- weight_out: bfloat16 [128, 1024], replicated, may hold values from -0.1875 to 0.1875
Outputs:
- final_state: float32 [4, 128, 16, 512], P('dp', None, 'lat', 'lon')
- state_grad: float32 [4, 128, 16, 512], P('dp', None, 'lat', 'lon')
- grad_in: float32 [1024, 128], replicated
- grad_out: float32 [128, 1024], replicated
All inputs are finite; a program needn't handle non-finite values.
Results may differ from a plain program's by a relative error of at most 0.006.
Values sent between devices are 32-bit elements; how exact they have to be, the bound alone decides.
A program may use at most 64 MiB of HBM per device.

v0:
```python
import math
import jax
import jax.numpy as jnp
from jax import lax
from jax.sharding import PartitionSpec as P

ROLL = 2
EPSILON = 1e-05
CONTRACT_LAST = (((1,), (1,)), ((), ()))
CONTRACT_FIRST = (((0,), (0,)), ((), ()))


def with_halo(block, sides, width, periodic):
    for axis, dim in sides:
        count = lax.axis_size(axis)
        forward = [(i, i + 1) for i in range(count - 1)]
        if periodic:
            forward.append((count - 1, 0))
        backward = [(target, source) for source, target in forward]
        low = lax.ppermute(
            lax.slice_in_dim(block, block.shape[dim] - width, None, axis=dim), axis, forward
        )
        high = lax.ppermute(lax.slice_in_dim(block, 0, width, axis=dim), axis, backward)
        block = jnp.concatenate([low, block, high], axis=dim)
    return block


def laplace(field):
    rows_ext = with_halo(field, (("lat", 1),), 1, False)
    cols_ext = with_halo(field, (("lon", 2),), 1, True)
    return (
        rows_ext[:, 2:, :]
        + rows_ext[:, :-2, :]
        + cols_ext[:, :, 2:]
        + cols_ext[:, :, :-2]
        - 4.0 * field
    )


def diffuse(field, diffusion):
    return field + diffusion[:, None, None] * laplace(field)


def physics(mixed, norm_gain, weight_in, bias_in, weight_out):
    inverse = lax.rsqrt(jnp.mean(mixed * mixed, axis=0) + EPSILON)
    normed = (mixed * inverse * norm_gain[:, None, None]).astype(jnp.bfloat16)
    flat_normed = normed.reshape(normed.shape[0], -1)
    pre_act = jnp.dot(weight_in, flat_normed, preferred_element_type=jnp.float32) + bias_in[:, None]
    squashed = jnp.tanh(pre_act)
    hidden = squashed.astype(jnp.bfloat16)
    update = jnp.dot(weight_out, hidden, preferred_element_type=jnp.float32)
    return (mixed + update.reshape(mixed.shape), (inverse, flat_normed, squashed, hidden))


def on_device(initial_state, cotangent, diffusion, norm_gain, weight_in, bias_in, weight_out):
    field = initial_state[0]
    channels = field.shape[0]
    saved_fields = []
    saved_mixed = []
    for section in range(ROLL):
        mixed = diffuse(field, diffusion)
        saved_fields.append(field)
        saved_mixed.append(mixed)
        field, unused = physics(mixed, norm_gain, weight_in, bias_in, weight_out)
    adjoint = cotangent[0]
    sum_in = jnp.zeros(weight_in.shape, jnp.float32)
    sum_out = jnp.zeros(weight_out.shape, jnp.float32)
    for section in reversed(range(ROLL)):
        mixed = diffuse(saved_fields[section], diffusion)
        unused, cache = physics(mixed, norm_gain, weight_in, bias_in, weight_out)
        inverse, flat_normed, squashed, hidden = cache
        adjoint_flat = adjoint.reshape(channels, -1).astype(jnp.bfloat16)
        term_out = lax.dot_general(
            adjoint_flat, hidden, CONTRACT_LAST, preferred_element_type=jnp.float32
        )
        hidden_adj = lax.dot_general(
            weight_out, adjoint_flat, CONTRACT_FIRST, preferred_element_type=jnp.float32
        )
        pre_adj = (hidden_adj * (1.0 - squashed * squashed)).astype(jnp.bfloat16)
        term_in = lax.dot_general(
            pre_adj, flat_normed, CONTRACT_LAST, preferred_element_type=jnp.float32
        )
        sum_in = sum_in + term_in
        sum_out = sum_out + term_out
        normed_adj = lax.dot_general(
            weight_in, pre_adj, CONTRACT_FIRST, preferred_element_type=jnp.float32
        )
        scaled_adj = normed_adj.reshape(mixed.shape) * norm_gain[:, None, None]
        inner = jnp.sum(scaled_adj * mixed, axis=0)
        mixed_adj = adjoint + inverse * scaled_adj - mixed * inverse**3 * inner / channels
        adjoint = mixed_adj + diffusion[:, None, None] * laplace(mixed_adj)
    sum_in, sum_out = lax.psum((sum_in, sum_out), ("dp", "lat", "lon"))
    columns_all = (
        lax.axis_size("dp")
        * lax.axis_size("lat")
        * lax.axis_size("lon")
        * field.shape[1]
        * field.shape[2]
    )
    factor = jnp.float32(1.0 / math.sqrt(columns_all))
    return (field[None], adjoint[None], sum_in * factor, sum_out * factor)


def solution(mesh):
    in_specs = (P("dp", None, "lat", "lon"), P("dp", None, "lat", "lon"), P(), P(), P(), P(), P())
    out_specs = (P("dp", None, "lat", "lon"), P("dp", None, "lat", "lon"), P(), P())
    return jax.shard_map(
        on_device, mesh=mesh, in_specs=in_specs, out_specs=out_specs, check_vma=False
    )
```

profile of v0, /device:TPU:0, one launch (start us, length us, event | category | flops | bytes accessed | tf_op | source)
XLA Modules:
  0.0 245.7 jit_solution(16050792861114076286)
XLA Ops:
  7.2 1.4 fusion.66
  8.6 1.3 collective-permute-start
  9.9 4.8 %collective-permute-start.1 = (f32[128,1,128]{2,1,0:T(1,128)S(1)}, f32[128,1,128]{2,1,0:T(1,128)S(1)}, u32[]{:S(2)}, u32[]{:S(2)}) collective-permute-start(f32[128,1,128]{2,1,0:T(1,128)S(1)} %get-tuple-element.31), channel_id=1, source_target_pairs={{0,4},{1,5},{2,6},{3,7},{8,12},{9,13},{10,14},{11,15},{16,20},{17,... | collective-permute-start | bytes 196616 | tf_op jit(solution)/shard_map/ppermute | solution.py:20
  14.8 1.4 fusion.67
  16.2 1.6 collective-permute-start.2
  17.8 11.8 %collective-permute-done.2 = f32[128,8,1]{2,1,0:T(8,128)S(1)} collective-permute-done((f32[128,8,1]{2,1,0:T(8,128)S(1)}, f32[128,8,1]{2,1,0:T(8,128)S(1)}, u32[]{:S(2)}, u32[]{:S(2)}) %collective-permute-start.2) | collective-permute-done | bytes 4128 | tf_op jit(solution)/shard_map/ppermute | solution.py:23
  29.5 2.1 collective-permute-done.3
  31.7 2.6 %multiply_reduce_fusion.3 = (f32[8,128]{1,0:T(8,128)S(1)}, f32[128,8,128]{2,1,0:T(8,128)S(1)}) fusion(f32[128,8,128]{2,1,0:T(8,128)} %bitcast.68, f32[128,8,1]{2,1,0:T(8,128)S(1)} %collective-permute-done.3, f32[128,8,1]{2,1,0:T(8,128)S(1)} %collective-permute-done.2, f32[128,1,128]{2,1,0:T(1,128)S(1)} %collective-permute-done.1, ...), kind=kLoop, calls=%fused_computation.63 | loop fusion | flops 1702912 | bytes 1192448 | tf_op jit(solution)/shard_map/reduce_sum | solution.py:45
  36.0 2.0 copy-done.1
  39.1 1.3 collective-permute-start.4
  40.4 4.5 %collective-permute-start.5 = (f32[128,1,128]{2,1,0:T(1,128)S(1)}, f32[128,1,128]{2,1,0:T(1,128)S(1)}, u32[]{:S(2)}, u32[]{:S(2)}) collective-permute-start(f32[128,1,128]{2,1,0:T(1,128)S(1)} %get-tuple-element.27), channel_id=1, source_target_pairs={{0,4},{1,5},{2,6},{3,7},{8,12},{9,13},{10,14},{11,15},{16,20},{17,... | collective-permute-start | bytes 196616 | tf_op jit(solution)/shard_map/ppermute | solution.py:20
  46.5 10.8 %collective-permute-done.6 = f32[128,8,1]{2,1,0:T(8,128)S(1)} collective-permute-done((f32[128,8,1]{2,1,0:T(8,128)S(1)}, f32[128,8,1]{2,1,0:T(8,128)S(1)}, u32[]{:S(2)}, u32[]{:S(2)}) %collective-permute-start.6) | collective-permute-done | bytes 4128 | tf_op jit(solution)/shard_map/ppermute | solution.py:23
  57.3 1.6 collective-permute-done.7
  61.2 2.0 copy-done.3
  65.0 3.2 %fusion = bf16[1024,1024]{0,1:T(8,128)(2,1)S(1)} fusion(f32[1024,1024]{1,0:T(8,128)} %copy-done.3, bf16[128,1024]{1,0:T(8,128)(2,1)S(1)} %copy-done, f32[1024]{0:T(1024)S(1)} %copy-done.13, bf16[16,8,8,128]{3,2,1,0:T(8,128)(2,1)} %bitcast.69), kind=kOutput, calls=%fused_computation.1 | convolution fusion | flops 273678336 | bytes 6819840 | tf_op jit(solution)/shard_map/dot_general | solution.py:76
  68.2 2.5 fusion.68
  70.7 2.0 copy.14
  72.7 1.3 multiply_reduce_fusion.1
  74.0 2.3 fusion.36
  76.6 1.6 collective-permute-start.8
  78.2 4.5 %collective-permute-start.9 = (f32[128,1,128]{2,1,0:T(1,128)S(1)}, f32[128,1,128]{2,1,0:T(1,128)S(1)}, u32[]{:S(2)}, u32[]{:S(2)}) collective-permute-start(f32[128,1,128]{2,1,0:T(1,128)S(1)} %get-tuple-element.21), channel_id=1, source_target_pairs={{0,4},{1,5},{2,6},{3,7},{8,12},{9,13},{10,14},{11,15},{16,20},{17,... | collective-permute-start | bytes 196616 | tf_op jit(solution)/shard_map/ppermute | solution.py:20
  84.0 10.3 %collective-permute-done.10 = f32[128,8,1]{2,1,0:T(8,128)S(1)} collective-permute-done((f32[128,8,1]{2,1,0:T(8,128)S(1)}, f32[128,8,1]{2,1,0:T(8,128)S(1)}, u32[]{:S(2)}, u32[]{:S(2)}) %collective-permute-start.10) | collective-permute-done | bytes 4128 | tf_op jit(solution)/shard_map/ppermute | solution.py:23
  94.3 2.4 collective-permute-done.11
  100.6 1.6 fusion.3
  102.9 1.5 convolution_add_fusion
  105.2 1.3 collective-permute-start.12
  106.5 4.5 %collective-permute-start.13 = (f32[128,1,128]{2,1,0:T(1,128)S(1)}, f32[128,1,128]{2,1,0:T(1,128)S(1)}, u32[]{:S(2)}, u32[]{:S(2)}) collective-permute-start(f32[128,1,128]{2,1,0:T(1,128)S(1)} %get-tuple-element.17), channel_id=1, source_target_pairs={{0,4},{1,5},{2,6},{3,7},{8,12},{9,13},{10,14},{11,15},{16,20},{17,... | collective-permute-start | bytes 196616 | tf_op jit(solution)/shard_map/ppermute | solution.py:20
  111.9 12.9 %collective-permute-done.14 = f32[128,8,1]{2,1,0:T(8,128)S(1)} collective-permute-done((f32[128,8,1]{2,1,0:T(8,128)S(1)}, f32[128,8,1]{2,1,0:T(8,128)S(1)}, u32[]{:S(2)}, u32[]{:S(2)}) %collective-permute-start.14) | collective-permute-done | bytes 4128 | tf_op jit(solution)/shard_map/ppermute | solution.py:23
  124.8 1.6 collective-permute-done.15
  126.4 1.4 fusion.15
  127.8 107.1 %all-reduce.3.cloned.1.call-done = (f32[1024,128]{1,0:T(8,128)}, f32[128,1024]{0,1:T(8,128)}) async-done(((f32[1024,128]{1,0:T(8,128)}, f32[128,1024]{0,1:T(8,128)}), (f32[1024,128]{1,0:T(8,128)}, f32[128,1024]{0,1:T(8,128)})) %all-reduce.3.cloned.1.call-update) | async-done | bytes 1048592 | tf_op jit(solution)/shard_map/psum | solution.py:92
  234.9 1.9 broadcast_multiply_fusion.1
  (76 shorter events, 18.0 us)
Async XLA Ops:
  7.2 30.8 %copy-start = (bf16[128,1024]{1,0:T(8,128)(2,1)S(1)}, bf16[128,1024]{1,0:T(8,128)(2,1)}, u32[]{:S(2)}) copy-start(bf16[128,1024]{1,0:T(8,128)(2,1)} %param.13) | copy-start | bytes 786436
  7.2 27.2 %copy-start.14 = (f32[128]{0:T(128)S(1)}, f32[128]{0:T(128)}, u32[]{:S(2)}) copy-start(f32[128]{0:T(128)} %param.10) | copy-start | bytes 1540
  7.2 28.1 %copy-start.5 = (bf16[1024,128]{1,0:T(8,128)(2,1)S(1)}, bf16[1024,128]{1,0:T(8,128)(2,1)}, u32[]{:S(2)}) copy-start(bf16[1024,128]{1,0:T(8,128)(2,1)} %param.11) | copy-start | bytes 786436
  7.2 227.7 %all-reduce.3.cloned.1.call-start = ((), (), s32[]{:S(2)}) async-start(), calls=%async_computation | async-start | bytes 2097152 | tf_op jit(solution)/shard_map/psum | solution.py:92
  8.6 23.1 %collective-permute-start = (f32[128,1,128]{2,1,0:T(1,128)S(1)}, f32[128,1,128]{2,1,0:T(1,128)S(1)}, u32[]{:S(2)}, u32[]{:S(2)}) collective-permute-start(f32[128,1,128]{2,1,0:T(1,128)S(1)} %get-tuple-element.30), channel_id=1, source_target_pairs={{4,0},{5,1},{6,2},{7,3},{12,8},{13,9},{14,10},{15,11},{20,16},{21,... | collective-permute-start | bytes 196616 | tf_op jit(solution)/shard_map/ppermute | solution.py:23
  9.9 21.8 %collective-permute-start.1 = (f32[128,1,128]{2,1,0:T(1,128)S(1)}, f32[128,1,128]{2,1,0:T(1,128)S(1)}, u32[]{:S(2)}, u32[]{:S(2)}) collective-permute-start(f32[128,1,128]{2,1,0:T(1,128)S(1)} %get-tuple-element.31), channel_id=1, source_target_pairs={{0,4},{1,5},{2,6},{3,7},{8,12},{9,13},{10,14},{11,15},{16,20},{17,... | collective-permute-start | bytes 196616 | tf_op jit(solution)/shard_map/ppermute | solution.py:20
  16.2 21.8 %copy-start.13 = (f32[1024]{0:T(1024)S(1)}, f32[1024]{0:T(1024)}, u32[]{:S(2)}) copy-start(f32[1024]{0:T(1024)} %param.12) | copy-start | bytes 12292
  16.2 13.4 %collective-permute-start.2 = (f32[128,8,1]{2,1,0:T(8,128)S(1)}, f32[128,8,1]{2,1,0:T(8,128)S(1)}, u32[]{:S(2)}, u32[]{:S(2)}) collective-permute-start(f32[128,8,1]{2,1,0:T(8,128)S(1)} %get-tuple-element.32), channel_id=1, source_target_pairs={{1,0},{2,1},{3,2},{0,3},{5,4},{6,5},{7,6},{4,7},{9,8},{10,9},{11,1... | collective-permute-start | bytes 12296 | tf_op jit(solution)/shard_map/ppermute | solution.py:23
  17.8 13.9 %collective-permute-start.3 = (f32[128,8,1]{2,1,0:T(8,128)S(1)}, f32[128,8,1]{2,1,0:T(8,128)S(1)}, u32[]{:S(2)}, u32[]{:S(2)}) collective-permute-start(f32[128,8,1]{2,1,0:T(8,128)S(1)} %get-tuple-element.33), channel_id=1, source_target_pairs={{0,1},{1,2},{2,3},{3,0},{4,5},{5,6},{6,7},{7,4},{8,9},{9,10},{10,1... | collective-permute-start | bytes 12296 | tf_op jit(solution)/shard_map/ppermute | solution.py:20
  34.6 0.7 copy-start.8
  36.0 2.0 copy-start.1
  38.0 7.8 %copy-start.12 = (f32[1,128,8,128]{3,2,1,0:T(8,128)S(1)}, f32[1,128,8,128]{3,2,1,0:T(8,128)}, u32[]{:S(2)}) copy-start(f32[1,128,8,128]{3,2,1,0:T(8,128)} %param.8) | copy-start | bytes 1572868
  38.0 20.9 %copy-start.15 = (f32[128]{0:T(128)S(1)}, f32[128]{0:T(128)}, u32[]{:S(2)}) copy-start(f32[128]{0:T(128)} %param.9) | copy-start | bytes 1540
  39.1 19.8 %collective-permute-start.4 = (f32[128,1,128]{2,1,0:T(1,128)S(1)}, f32[128,1,128]{2,1,0:T(1,128)S(1)}, u32[]{:S(2)}, u32[]{:S(2)}) collective-permute-start(f32[128,1,128]{2,1,0:T(1,128)S(1)} %get-tuple-element.26), channel_id=1, source_target_pairs={{4,0},{5,1},{6,2},{7,3},{12,8},{13,9},{14,10},{15,11},{20,16},{21,... | collective-permute-start | bytes 196616 | tf_op jit(solution)/shard_map/ppermute | solution.py:23
  40.4 18.5 %collective-permute-start.5 = (f32[128,1,128]{2,1,0:T(1,128)S(1)}, f32[128,1,128]{2,1,0:T(1,128)S(1)}, u32[]{:S(2)}, u32[]{:S(2)}) collective-permute-start(f32[128,1,128]{2,1,0:T(1,128)S(1)} %get-tuple-element.27), channel_id=1, source_target_pairs={{0,4},{1,5},{2,6},{3,7},{8,12},{9,13},{10,14},{11,15},{16,20},{17,... | collective-permute-start | bytes 196616 | tf_op jit(solution)/shard_map/ppermute | solution.py:20
  45.2 12.1 %collective-permute-start.6 = (f32[128,8,1]{2,1,0:T(8,128)S(1)}, f32[128,8,1]{2,1,0:T(8,128)S(1)}, u32[]{:S(2)}, u32[]{:S(2)}) collective-permute-start(f32[128,8,1]{2,1,0:T(8,128)S(1)} %get-tuple-element.28), channel_id=1, source_target_pairs={{1,0},{2,1},{3,2},{0,3},{5,4},{6,5},{7,6},{4,7},{9,8},{10,9},{11,1... | collective-permute-start | bytes 12296 | tf_op jit(solution)/shard_map/ppermute | solution.py:23
  45.3 13.7 %collective-permute-start.7 = (f32[128,8,1]{2,1,0:T(8,128)S(1)}, f32[128,8,1]{2,1,0:T(8,128)S(1)}, u32[]{:S(2)}, u32[]{:S(2)}) collective-permute-start(f32[128,8,1]{2,1,0:T(8,128)S(1)} %get-tuple-element.29), channel_id=1, source_target_pairs={{0,1},{1,2},{2,3},{3,0},{4,5},{5,6},{6,7},{7,4},{8,9},{9,10},{10,1... | collective-permute-start | bytes 12296 | tf_op jit(solution)/shard_map/ppermute | solution.py:20
  61.2 2.0 copy-start.3
  72.7 10.6 %copy-start.11 = (bf16[128,8,128]{2,1,0:T(8,128)(2,1)S(1)}, bf16[128,8,128]{2,1,0:T(8,128)(2,1)}, u32[]{:S(2)}) copy-start(bf16[128,8,128]{2,1,0:T(8,128)(2,1)} %copy-done.10) | copy-start | bytes 786436
  76.6 20.7 %copy-start.2 = (f32[1024,1024]{1,0:T(8,128)S(1)}, f32[1024,1024]{1,0:T(8,128)}, u32[]{:S(2)}) copy-start(f32[1024,1024]{1,0:T(8,128)} %copy-done.1) | copy-start | bytes 12582916
  76.6 20.1 %collective-permute-start.8 = (f32[128,1,128]{2,1,0:T(1,128)S(1)}, f32[128,1,128]{2,1,0:T(1,128)S(1)}, u32[]{:S(2)}, u32[]{:S(2)}) collective-permute-start(f32[128,1,128]{2,1,0:T(1,128)S(1)} %get-tuple-element.20), channel_id=1, source_target_pairs={{4,0},{5,1},{6,2},{7,3},{12,8},{13,9},{14,10},{15,11},{20,16},{21,... | collective-permute-start | bytes 196616 | tf_op jit(solution)/shard_map/ppermute | solution.py:23
  78.2 18.5 %collective-permute-start.9 = (f32[128,1,128]{2,1,0:T(1,128)S(1)}, f32[128,1,128]{2,1,0:T(1,128)S(1)}, u32[]{:S(2)}, u32[]{:S(2)}) collective-permute-start(f32[128,1,128]{2,1,0:T(1,128)S(1)} %get-tuple-element.21), channel_id=1, source_target_pairs={{0,4},{1,5},{2,6},{3,7},{8,12},{9,13},{10,14},{11,15},{16,20},{17,... | collective-permute-start | bytes 196616 | tf_op jit(solution)/shard_map/ppermute | solution.py:20
  82.7 11.6 %collective-permute-start.10 = (f32[128,8,1]{2,1,0:T(8,128)S(1)}, f32[128,8,1]{2,1,0:T(8,128)S(1)}, u32[]{:S(2)}, u32[]{:S(2)}) collective-permute-start(f32[128,8,1]{2,1,0:T(8,128)S(1)} %get-tuple-element.22), channel_id=1, source_target_pairs={{1,0},{2,1},{3,2},{0,3},{5,4},{6,5},{7,6},{4,7},{9,8},{10,9},{11,1... | collective-permute-start | bytes 12296 | tf_op jit(solution)/shard_map/ppermute | solution.py:23
  82.8 13.9 %collective-permute-start.11 = (f32[128,8,1]{2,1,0:T(8,128)S(1)}, f32[128,8,1]{2,1,0:T(8,128)S(1)}, u32[]{:S(2)}, u32[]{:S(2)}) collective-permute-start(f32[128,8,1]{2,1,0:T(8,128)S(1)} %get-tuple-element.23), channel_id=1, source_target_pairs={{0,1},{1,2},{2,3},{3,0},{4,5},{5,6},{6,7},{7,4},{8,9},{9,10},{10,1... | collective-permute-start | bytes 12296 | tf_op jit(solution)/shard_map/ppermute | solution.py:20
  98.3 2.2 copy-start.4
  98.3 2.2 copy-start.7
  100.6 1.6 copy-start.6
  100.6 2.4 copy-start.9
  105.2 21.2 %collective-permute-start.12 = (f32[128,1,128]{2,1,0:T(1,128)S(1)}, f32[128,1,128]{2,1,0:T(1,128)S(1)}, u32[]{:S(2)}, u32[]{:S(2)}) collective-permute-start(f32[128,1,128]{2,1,0:T(1,128)S(1)} %get-tuple-element.16), channel_id=1, source_target_pairs={{4,0},{5,1},{6,2},{7,3},{12,8},{13,9},{14,10},{15,11},{20,16},{21,... | collective-permute-start | bytes 196616 | tf_op jit(solution)/shard_map/ppermute | solution.py:23
  106.5 19.9 %collective-permute-start.13 = (f32[128,1,128]{2,1,0:T(1,128)S(1)}, f32[128,1,128]{2,1,0:T(1,128)S(1)}, u32[]{:S(2)}, u32[]{:S(2)}) collective-permute-start(f32[128,1,128]{2,1,0:T(1,128)S(1)} %get-tuple-element.17), channel_id=1, source_target_pairs={{0,4},{1,5},{2,6},{3,7},{8,12},{9,13},{10,14},{11,15},{16,20},{17,... | collective-permute-start | bytes 196616 | tf_op jit(solution)/shard_map/ppermute | solution.py:20
  111.3 13.5 %collective-permute-start.14 = (f32[128,8,1]{2,1,0:T(8,128)S(1)}, f32[128,8,1]{2,1,0:T(8,128)S(1)}, u32[]{:S(2)}, u32[]{:S(2)}) collective-permute-start(f32[128,8,1]{2,1,0:T(8,128)S(1)} %get-tuple-element.18), channel_id=1, source_target_pairs={{1,0},{2,1},{3,2},{0,3},{5,4},{6,5},{7,6},{4,7},{9,8},{10,9},{11,1... | collective-permute-start | bytes 12296 | tf_op jit(solution)/shard_map/ppermute | solution.py:23
  111.4 15.1 %collective-permute-start.15 = (f32[128,8,1]{2,1,0:T(8,128)S(1)}, f32[128,8,1]{2,1,0:T(8,128)S(1)}, u32[]{:S(2)}, u32[]{:S(2)}) collective-permute-start(f32[128,8,1]{2,1,0:T(8,128)S(1)} %get-tuple-element.19), channel_id=1, source_target_pairs={{0,1},{1,2},{2,3},{3,0},{4,5},{5,6},{6,7},{7,4},{8,9},{9,10},{10,1... | collective-permute-start | bytes 12296 | tf_op jit(solution)/shard_map/ppermute | solution.py:20
  (1 other events, 0.7 us)
Sparse Core Ops, SparseCore 0:
  105.1 129.8 all-reduce.2
where the time goes:
time: 246 us
  waiting for transfers between devices  161 us (65%)
  starting transfers between devices  27.2 us (11%)
  matrix products  15.2 us (6%)
  local copies, waits for them, and re-layouts  14.8 us (6%)
  between operations  14.4 us (6%)
  other arithmetic  13.5 us (5%)
    psum x1, waiting for transfers between devices, on_device(): sum_in, sum_out = lax.psum((sum_in, sum_out), ('dp', 'lat', 'lon'))  107 us
    ppermute x8, waiting for transfers between devices, with_halo(): lax.ppermute(lax.slice_in_dim(block, 0, width, axis=dim), axis, backward)  45.8 us
    ppermute x8, starting transfers between devices, with_halo(): lax.ppermute(lax.slice_in_dim(block, block.shape[dim] - width, None, axis...  20 us
    ppermute x8, waiting for transfers between devices, with_halo(): lax.ppermute(lax.slice_in_dim(block, block.shape[dim] - width, None, axis...  7.8 us
    unnamed x33, local copies, waits for them, and re-layouts  7.67 us
    ppermute x8, starting transfers between devices, with_halo(): lax.ppermute(lax.slice_in_dim(block, 0, width, axis=dim), axis, backward)  7.2 us
  transfers between devices with their start and end apart: 17, of which 9 were waited for; matrix products, arithmetic and copies ran while one was open for 2% of the time, Pallas kernels for 0%

commit v1 on v0

--- a/solution.py
+++ b/solution.py
@@ -89,7 +89,7 @@
         inner = jnp.sum(scaled_adj * mixed, axis=0)
         mixed_adj = adjoint + inverse * scaled_adj - mixed * inverse**3 * inner / channels
         adjoint = mixed_adj + diffusion[:, None, None] * laplace(mixed_adj)
-    sum_in, sum_out = lax.psum((sum_in, sum_out), ("dp", "lat", "lon"))
+    sum_in, sum_out = lax.psum(lax.psum((sum_in, sum_out), ("lat", "lon")), "dp")
     columns_all = (
         lax.axis_size("dp")
         * lax.axis_size("lat")

time: 246 us -> 226 us (0.919)
  waiting for transfers between devices: 161 us -> 137 us
    psum x1 -> x2, waiting for transfers between devices: 107 us -> 85 us  [the longest x1 53.7 us: on_device(): lax.psum((sum_in, sum_out), ('lat', 'lon'))]
  transfers between devices with their start and end apart: 17 -> 18, of which waited for: 9 -> 10; matrix products, arithmetic and copies ran while one was open for 2% -> 4% of each run, Pallas kernels for 0% -> 0%
where the time goes in v1:
time: 226 us
  waiting for transfers between devices  137 us (61%)
  starting transfers between devices  27.3 us (12%)
  matrix products  16 us (7%)
  local copies, waits for them, and re-layouts  15.8 us (7%)
  other arithmetic  15.4 us (7%)
  between operations  14.4 us (6%)
    psum x1, waiting for transfers between devices, on_device(): lax.psum((sum_in, sum_out), ('lat', 'lon'))  53.7 us
    ppermute x8, waiting for transfers between devices, with_halo(): lax.ppermute(lax.slice_in_dim(block, 0, width, axis=dim), axis, backward)  44.6 us
    psum x1, waiting for transfers between devices, on_device(): lax.psum(lax.psum((sum_in, sum_out), ('lat', 'lon')), 'dp')  31.3 us
    ppermute x8, starting transfers between devices, with_halo(): lax.ppermute(lax.slice_in_dim(block, block.shape[dim] - width, None, axis...  20 us
    unnamed x33, local copies, waits for them, and re-layouts  7.64 us
    ppermute x8, starting transfers between devices, with_halo(): lax.ppermute(lax.slice_in_dim(block, 0, width, axis=dim), axis, backward)  7.2 us
    ppermute x8, waiting for transfers between devices, with_halo(): lax.ppermute(lax.slice_in_dim(block, block.shape[dim] - width, None, axis...  7.11 us
  transfers between devices with their start and end apart: 18, of which 10 were waited for; matrix products, arithmetic and copies ran while one was open for 4% of the time, Pallas kernels for 0%

profile of v1, /device:TPU:0, one launch (start us, length us, event | category | flops | bytes accessed | tf_op | source)
XLA Modules:
  0.0 225.7 jit_solution(11211050244715881305)
XLA Ops:
  7.2 1.4 fusion.66
  8.6 1.3 collective-permute-start
  9.9 4.8 %collective-permute-start.1 = (f32[128,1,128]{2,1,0:T(1,128)S(1)}, f32[128,1,128]{2,1,0:T(1,128)S(1)}, u32[]{:S(2)}, u32[]{:S(2)}) collective-permute-start(f32[128,1,128]{2,1,0:T(1,128)S(1)} %get-tuple-element.33), channel_id=1, source_target_pairs={{0,4},{1,5},{2,6},{3,7},{8,12},{9,13},{10,14},{11,15},{16,20},{17,... | collective-permute-start | bytes 196616 | tf_op jit(solution)/shard_map/ppermute | solution.py:20
  14.8 1.4 fusion.67
  16.2 1.6 collective-permute-start.2
  17.8 11.8 %collective-permute-done.2 = f32[128,8,1]{2,1,0:T(8,128)S(1)} collective-permute-done((f32[128,8,1]{2,1,0:T(8,128)S(1)}, f32[128,8,1]{2,1,0:T(8,128)S(1)}, u32[]{:S(2)}, u32[]{:S(2)}) %collective-permute-start.2) | collective-permute-done | bytes 4128 | tf_op jit(solution)/shard_map/ppermute | solution.py:23
  29.6 2.1 collective-permute-done.3
  31.7 2.7 %multiply_reduce_fusion.3 = (f32[8,128]{1,0:T(8,128)S(1)}, f32[128,8,128]{2,1,0:T(8,128)S(1)}) fusion(f32[128,8,128]{2,1,0:T(8,128)} %bitcast.68, f32[128,8,1]{2,1,0:T(8,128)S(1)} %collective-permute-done.3, f32[128,8,1]{2,1,0:T(8,128)S(1)} %collective-permute-done.2, f32[128,1,128]{2,1,0:T(1,128)S(1)} %collective-permute-done.1, ...), kind=kLoop, calls=%fused_computation.63 | loop fusion | flops 1702912 | bytes 1192448 | tf_op jit(solution)/shard_map/reduce_sum | solution.py:45
  36.2 2.0 copy-done.1
  39.3 1.3 collective-permute-start.4
  40.6 4.5 %collective-permute-start.5 = (f32[128,1,128]{2,1,0:T(1,128)S(1)}, f32[128,1,128]{2,1,0:T(1,128)S(1)}, u32[]{:S(2)}, u32[]{:S(2)}) collective-permute-start(f32[128,1,128]{2,1,0:T(1,128)S(1)} %get-tuple-element.29), channel_id=1, source_target_pairs={{0,4},{1,5},{2,6},{3,7},{8,12},{9,13},{10,14},{11,15},{16,20},{17,... | collective-permute-start | bytes 196616 | tf_op jit(solution)/shard_map/ppermute | solution.py:20
  46.6 10.8 %collective-permute-done.6 = f32[128,8,1]{2,1,0:T(8,128)S(1)} collective-permute-done((f32[128,8,1]{2,1,0:T(8,128)S(1)}, f32[128,8,1]{2,1,0:T(8,128)S(1)}, u32[]{:S(2)}, u32[]{:S(2)}) %collective-permute-start.6) | collective-permute-done | bytes 4128 | tf_op jit(solution)/shard_map/ppermute | solution.py:23
  57.4 1.7 collective-permute-done.7
  61.4 2.0 copy-done.3
  65.1 3.2 %fusion = bf16[1024,1024]{0,1:T(8,128)(2,1)S(1)} fusion(f32[1024,1024]{1,0:T(8,128)} %copy-done.3, bf16[128,1024]{1,0:T(8,128)(2,1)S(1)} %copy-done, f32[1024]{0:T(1024)S(1)} %copy-done.13, bf16[16,8,8,128]{3,2,1,0:T(8,128)(2,1)} %bitcast.69), kind=kOutput, calls=%fused_computation.1 | convolution fusion | flops 273678336 | bytes 6819840 | tf_op jit(solution)/shard_map/dot_general | solution.py:76
  68.4 2.5 %fusion.68 = f32[1024,128]{1,0:T(8,128)} fusion(bf16[1024,1024]{0,1:T(8,128)(2,1)S(1)} %fusion, bf16[1024,128]{1,0:T(8,128)(2,1)} %param.11), kind=kOutput, calls=%fused_computation.98 | convolution fusion | flops 268435456 | bytes 2883584 | tf_op jit(solution)/shard_map/dot_general | solution.py:85
  70.8 2.0 copy.14
  74.1 2.3 %fusion.36 = (f32[128,8,128]{2,1,0:T(8,128)S(1)}, f32[1,128,8,128]{3,2,1,0:T(8,128)}) fusion(f32[1,128,8,128]{3,2,1,0:T(8,128)} %param.8, f32[128,8,128]{2,1,0:T(8,128)S(1)} %get-tuple-element.15, f32[128,8,128]{2,1,0:T(8,128)} %copy.14, f32[8,128]{1,0:T(8,128)S(1)} %multiply_reduce_fusion.1, f32[8,128]{1,0:T(8,128)S(1)} %get-tuple-element.38, ...), kind=kLoop, calls=%fused_computation.55 | loop fusion | flops 1048576 | bytes 3158528 | tf_op jit(solution)/shard_map/sub | solution.py:90
  76.7 1.6 collective-permute-start.8
  78.3 4.5 %collective-permute-start.9 = (f32[128,1,128]{2,1,0:T(1,128)S(1)}, f32[128,1,128]{2,1,0:T(1,128)S(1)}, u32[]{:S(2)}, u32[]{:S(2)}) collective-permute-start(f32[128,1,128]{2,1,0:T(1,128)S(1)} %get-tuple-element.23), channel_id=1, source_target_pairs={{0,4},{1,5},{2,6},{3,7},{8,12},{9,13},{10,14},{11,15},{16,20},{17,... | collective-permute-start | bytes 196616 | tf_op jit(solution)/shard_map/ppermute | solution.py:20
  84.2 10.3 %collective-permute-done.10 = f32[128,8,1]{2,1,0:T(8,128)S(1)} collective-permute-done((f32[128,8,1]{2,1,0:T(8,128)S(1)}, f32[128,8,1]{2,1,0:T(8,128)S(1)}, u32[]{:S(2)}, u32[]{:S(2)}) %collective-permute-start.10) | collective-permute-done | bytes 4128 | tf_op jit(solution)/shard_map/ppermute | solution.py:23
  94.5 2.3 %collective-permute-done.11 = f32[128,8,1]{2,1,0:T(8,128)S(1)} collective-permute-done((f32[128,8,1]{2,1,0:T(8,128)S(1)}, f32[128,8,1]{2,1,0:T(8,128)S(1)}, u32[]{:S(2)}, u32[]{:S(2)}) %collective-permute-start.11) | collective-permute-done | bytes 4128 | tf_op jit(solution)/shard_map/ppermute | solution.py:20
  96.8 1.4 fusion.56
  101.4 1.6 fusion.3
  103.1 1.5 convolution_add_fusion
  104.7 1.5 fusion.69
  107.5 53.7 %all-reduce.5.cloned.1.call-done = (f32[1024,128]{1,0:T(8,128)}, f32[128,1024]{0,1:T(8,128)}) async-done(((f32[1024,128]{1,0:T(8,128)}, f32[128,1024]{0,1:T(8,128)}), (f32[1024,128]{1,0:T(8,128)}, f32[128,1024]{0,1:T(8,128)})) %all-reduce.5.cloned.1.call-update) | async-done | bytes 1048592 | tf_op jit(solution)/shard_map/psum | solution.py:92
  164.1 4.5 %collective-permute-start.13 = (f32[128,1,128]{2,1,0:T(1,128)S(1)}, f32[128,1,128]{2,1,0:T(1,128)S(1)}, u32[]{:S(2)}, u32[]{:S(2)}) collective-permute-start(f32[128,1,128]{2,1,0:T(1,128)S(1)} %get-tuple-element.19), channel_id=1, source_target_pairs={{0,4},{1,5},{2,6},{3,7},{8,12},{9,13},{10,14},{11,15},{16,20},{17,... | collective-permute-start | bytes 196616 | tf_op jit(solution)/shard_map/ppermute | solution.py:20
  169.4 11.8 %collective-permute-done.14 = f32[128,8,1]{2,1,0:T(8,128)S(1)} collective-permute-done((f32[128,8,1]{2,1,0:T(8,128)S(1)}, f32[128,8,1]{2,1,0:T(8,128)S(1)}, u32[]{:S(2)}, u32[]{:S(2)}) %collective-permute-start.14) | collective-permute-done | bytes 4128 | tf_op jit(solution)/shard_map/ppermute | solution.py:23
  182.2 1.4 fusion.15
  183.6 31.3 %all-reduce.7.cloned.1.call-done = (f32[1024,128]{1,0:T(8,128)}, f32[128,1024]{0,1:T(8,128)}) async-done(((f32[1024,128]{1,0:T(8,128)}, f32[128,1024]{0,1:T(8,128)}), (f32[1024,128]{1,0:T(8,128)}, f32[128,1024]{0,1:T(8,128)})) %all-reduce.7.cloned.1.call-update) | async-done | bytes 1048592 | tf_op jit(solution)/shard_map/psum | solution.py:92
  214.9 1.9 broadcast_multiply_fusion.1
  (79 shorter events, 22.4 us)
Async XLA Ops:
  7.2 31.0 %copy-start = (bf16[128,1024]{1,0:T(8,128)(2,1)S(1)}, bf16[128,1024]{1,0:T(8,128)(2,1)}, u32[]{:S(2)}) copy-start(bf16[128,1024]{1,0:T(8,128)(2,1)} %param.13) | copy-start | bytes 786436
  7.2 27.3 %copy-start.14 = (f32[128]{0:T(128)S(1)}, f32[128]{0:T(128)}, u32[]{:S(2)}) copy-start(f32[128]{0:T(128)} %param.10) | copy-start | bytes 1540
  7.2 28.2 %copy-start.5 = (bf16[1024,128]{1,0:T(8,128)(2,1)S(1)}, bf16[1024,128]{1,0:T(8,128)(2,1)}, u32[]{:S(2)}) copy-start(bf16[1024,128]{1,0:T(8,128)(2,1)} %param.11) | copy-start | bytes 786436
  7.2 154.0 %all-reduce.5.cloned.1.call-start = ((), (), s32[]{:S(2)}) async-start(), calls=%async_computation | async-start | bytes 2097152 | tf_op jit(solution)/shard_map/psum | solution.py:92
  8.6 23.1 %collective-permute-start = (f32[128,1,128]{2,1,0:T(1,128)S(1)}, f32[128,1,128]{2,1,0:T(1,128)S(1)}, u32[]{:S(2)}, u32[]{:S(2)}) collective-permute-start(f32[128,1,128]{2,1,0:T(1,128)S(1)} %get-tuple-element.32), channel_id=1, source_target_pairs={{4,0},{5,1},{6,2},{7,3},{12,8},{13,9},{14,10},{15,11},{20,16},{21,... | collective-permute-start | bytes 196616 | tf_op jit(solution)/shard_map/ppermute | solution.py:23
  9.9 21.8 %collective-permute-start.1 = (f32[128,1,128]{2,1,0:T(1,128)S(1)}, f32[128,1,128]{2,1,0:T(1,128)S(1)}, u32[]{:S(2)}, u32[]{:S(2)}) collective-permute-start(f32[128,1,128]{2,1,0:T(1,128)S(1)} %get-tuple-element.33), channel_id=1, source_target_pairs={{0,4},{1,5},{2,6},{3,7},{8,12},{9,13},{10,14},{11,15},{16,20},{17,... | collective-permute-start | bytes 196616 | tf_op jit(solution)/shard_map/ppermute | solution.py:20
  16.2 21.9 %copy-start.13 = (f32[1024]{0:T(1024)S(1)}, f32[1024]{0:T(1024)}, u32[]{:S(2)}) copy-start(f32[1024]{0:T(1024)} %param.12) | copy-start | bytes 12292
  16.2 13.4 %collective-permute-start.2 = (f32[128,8,1]{2,1,0:T(8,128)S(1)}, f32[128,8,1]{2,1,0:T(8,128)S(1)}, u32[]{:S(2)}, u32[]{:S(2)}) collective-permute-start(f32[128,8,1]{2,1,0:T(8,128)S(1)} %get-tuple-element.34), channel_id=1, source_target_pairs={{1,0},{2,1},{3,2},{0,3},{5,4},{6,5},{7,6},{4,7},{9,8},{10,9},{11,1... | collective-permute-start | bytes 12296 | tf_op jit(solution)/shard_map/ppermute | solution.py:23
  17.8 13.9 %collective-permute-start.3 = (f32[128,8,1]{2,1,0:T(8,128)S(1)}, f32[128,8,1]{2,1,0:T(8,128)S(1)}, u32[]{:S(2)}, u32[]{:S(2)}) collective-permute-start(f32[128,8,1]{2,1,0:T(8,128)S(1)} %get-tuple-element.35), channel_id=1, source_target_pairs={{0,1},{1,2},{2,3},{3,0},{4,5},{5,6},{6,7},{7,4},{8,9},{9,10},{10,1... | collective-permute-start | bytes 12296 | tf_op jit(solution)/shard_map/ppermute | solution.py:20
  36.2 2.0 copy-start.1
  38.1 7.8 %copy-start.12 = (f32[1,128,8,128]{3,2,1,0:T(8,128)S(1)}, f32[1,128,8,128]{3,2,1,0:T(8,128)}, u32[]{:S(2)}) copy-start(f32[1,128,8,128]{3,2,1,0:T(8,128)} %param.8) | copy-start | bytes 1572868
  38.1 20.9 %copy-start.15 = (f32[128]{0:T(128)S(1)}, f32[128]{0:T(128)}, u32[]{:S(2)}) copy-start(f32[128]{0:T(128)} %param.9) | copy-start | bytes 1540
  39.3 19.8 %collective-permute-start.4 = (f32[128,1,128]{2,1,0:T(1,128)S(1)}, f32[128,1,128]{2,1,0:T(1,128)S(1)}, u32[]{:S(2)}, u32[]{:S(2)}) collective-permute-start(f32[128,1,128]{2,1,0:T(1,128)S(1)} %get-tuple-element.28), channel_id=1, source_target_pairs={{4,0},{5,1},{6,2},{7,3},{12,8},{13,9},{14,10},{15,11},{20,16},{21,... | collective-permute-start | bytes 196616 | tf_op jit(solution)/shard_map/ppermute | solution.py:23
  40.6 18.5 %collective-permute-start.5 = (f32[128,1,128]{2,1,0:T(1,128)S(1)}, f32[128,1,128]{2,1,0:T(1,128)S(1)}, u32[]{:S(2)}, u32[]{:S(2)}) collective-permute-start(f32[128,1,128]{2,1,0:T(1,128)S(1)} %get-tuple-element.29), channel_id=1, source_target_pairs={{0,4},{1,5},{2,6},{3,7},{8,12},{9,13},{10,14},{11,15},{16,20},{17,... | collective-permute-start | bytes 196616 | tf_op jit(solution)/shard_map/ppermute | solution.py:20
  45.3 12.1 %collective-permute-start.6 = (f32[128,8,1]{2,1,0:T(8,128)S(1)}, f32[128,8,1]{2,1,0:T(8,128)S(1)}, u32[]{:S(2)}, u32[]{:S(2)}) collective-permute-start(f32[128,8,1]{2,1,0:T(8,128)S(1)} %get-tuple-element.30), channel_id=1, source_target_pairs={{1,0},{2,1},{3,2},{0,3},{5,4},{6,5},{7,6},{4,7},{9,8},{10,9},{11,1... | collective-permute-start | bytes 12296 | tf_op jit(solution)/shard_map/ppermute | solution.py:23
  45.4 13.7 %collective-permute-start.7 = (f32[128,8,1]{2,1,0:T(8,128)S(1)}, f32[128,8,1]{2,1,0:T(8,128)S(1)}, u32[]{:S(2)}, u32[]{:S(2)}) collective-permute-start(f32[128,8,1]{2,1,0:T(8,128)S(1)} %get-tuple-element.31), channel_id=1, source_target_pairs={{0,1},{1,2},{2,3},{3,0},{4,5},{5,6},{6,7},{7,4},{8,9},{9,10},{10,1... | collective-permute-start | bytes 12296 | tf_op jit(solution)/shard_map/ppermute | solution.py:20
  61.3 2.0 copy-start.3
  72.8 10.6 %copy-start.11 = (bf16[128,8,128]{2,1,0:T(8,128)(2,1)S(1)}, bf16[128,8,128]{2,1,0:T(8,128)(2,1)}, u32[]{:S(2)}) copy-start(bf16[128,8,128]{2,1,0:T(8,128)(2,1)} %copy-done.10) | copy-start | bytes 786436
  76.7 21.5 %copy-start.2 = (f32[1024,1024]{1,0:T(8,128)S(1)}, f32[1024,1024]{1,0:T(8,128)}, u32[]{:S(2)}) copy-start(f32[1024,1024]{1,0:T(8,128)} %copy-done.1) | copy-start | bytes 12582916
  76.7 20.1 %collective-permute-start.8 = (f32[128,1,128]{2,1,0:T(1,128)S(1)}, f32[128,1,128]{2,1,0:T(1,128)S(1)}, u32[]{:S(2)}, u32[]{:S(2)}) collective-permute-start(f32[128,1,128]{2,1,0:T(1,128)S(1)} %get-tuple-element.22), channel_id=1, source_target_pairs={{4,0},{5,1},{6,2},{7,3},{12,8},{13,9},{14,10},{15,11},{20,16},{21,... | collective-permute-start | bytes 196616 | tf_op jit(solution)/shard_map/ppermute | solution.py:23
  78.3 18.5 %collective-permute-start.9 = (f32[128,1,128]{2,1,0:T(1,128)S(1)}, f32[128,1,128]{2,1,0:T(1,128)S(1)}, u32[]{:S(2)}, u32[]{:S(2)}) collective-permute-start(f32[128,1,128]{2,1,0:T(1,128)S(1)} %get-tuple-element.23), channel_id=1, source_target_pairs={{0,4},{1,5},{2,6},{3,7},{8,12},{9,13},{10,14},{11,15},{16,20},{17,... | collective-permute-start | bytes 196616 | tf_op jit(solution)/shard_map/ppermute | solution.py:20
  82.8 11.6 %collective-permute-start.10 = (f32[128,8,1]{2,1,0:T(8,128)S(1)}, f32[128,8,1]{2,1,0:T(8,128)S(1)}, u32[]{:S(2)}, u32[]{:S(2)}) collective-permute-start(f32[128,8,1]{2,1,0:T(8,128)S(1)} %get-tuple-element.24), channel_id=1, source_target_pairs={{1,0},{2,1},{3,2},{0,3},{5,4},{6,5},{7,6},{4,7},{9,8},{10,9},{11,1... | collective-permute-start | bytes 12296 | tf_op jit(solution)/shard_map/ppermute | solution.py:23
  82.9 13.9 %collective-permute-start.11 = (f32[128,8,1]{2,1,0:T(8,128)S(1)}, f32[128,8,1]{2,1,0:T(8,128)S(1)}, u32[]{:S(2)}, u32[]{:S(2)}) collective-permute-start(f32[128,8,1]{2,1,0:T(8,128)S(1)} %get-tuple-element.25), channel_id=1, source_target_pairs={{0,1},{1,2},{2,3},{3,0},{4,5},{5,6},{6,7},{7,4},{8,9},{9,10},{10,1... | collective-permute-start | bytes 12296 | tf_op jit(solution)/shard_map/ppermute | solution.py:20
  99.2 2.2 copy-start.4
  99.2 2.2 copy-start.7
  101.4 1.7 copy-start.9
  103.1 1.6 copy-start.6
  104.7 110.2 %all-reduce.7.cloned.1.call-start = ((), (), s32[]{:S(2)}) async-start(), calls=%async_computation.1 | async-start | bytes 2097152 | tf_op jit(solution)/shard_map/psum | solution.py:92
  162.8 19.4 %collective-permute-start.12 = (f32[128,1,128]{2,1,0:T(1,128)S(1)}, f32[128,1,128]{2,1,0:T(1,128)S(1)}, u32[]{:S(2)}, u32[]{:S(2)}) collective-permute-start(f32[128,1,128]{2,1,0:T(1,128)S(1)} %get-tuple-element.18), channel_id=1, source_target_pairs={{4,0},{5,1},{6,2},{7,3},{12,8},{13,9},{14,10},{15,11},{20,16},{21,... | collective-permute-start | bytes 196616 | tf_op jit(solution)/shard_map/ppermute | solution.py:23
  164.1 18.1 %collective-permute-start.13 = (f32[128,1,128]{2,1,0:T(1,128)S(1)}, f32[128,1,128]{2,1,0:T(1,128)S(1)}, u32[]{:S(2)}, u32[]{:S(2)}) collective-permute-start(f32[128,1,128]{2,1,0:T(1,128)S(1)} %get-tuple-element.19), channel_id=1, source_target_pairs={{0,4},{1,5},{2,6},{3,7},{8,12},{9,13},{10,14},{11,15},{16,20},{17,... | collective-permute-start | bytes 196616 | tf_op jit(solution)/shard_map/ppermute | solution.py:20
  168.9 12.4 %collective-permute-start.14 = (f32[128,8,1]{2,1,0:T(8,128)S(1)}, f32[128,8,1]{2,1,0:T(8,128)S(1)}, u32[]{:S(2)}, u32[]{:S(2)}) collective-permute-start(f32[128,8,1]{2,1,0:T(8,128)S(1)} %get-tuple-element.20), channel_id=1, source_target_pairs={{1,0},{2,1},{3,2},{0,3},{5,4},{6,5},{7,6},{4,7},{9,8},{10,9},{11,1... | collective-permute-start | bytes 12296 | tf_op jit(solution)/shard_map/ppermute | solution.py:23
  168.9 13.3 %collective-permute-start.15 = (f32[128,8,1]{2,1,0:T(8,128)S(1)}, f32[128,8,1]{2,1,0:T(8,128)S(1)}, u32[]{:S(2)}, u32[]{:S(2)}) collective-permute-start(f32[128,8,1]{2,1,0:T(8,128)S(1)} %get-tuple-element.21), channel_id=1, source_target_pairs={{0,1},{1,2},{2,3},{3,0},{4,5},{5,6},{6,7},{7,4},{8,9},{9,10},{10,1... | collective-permute-start | bytes 12296 | tf_op jit(solution)/shard_map/ppermute | solution.py:20
  (2 other events, 1.4 us)
Sparse Core Ops, SparseCore 0:
  104.8 56.3 all-reduce.4
  163.6 51.2 all-reduce.6
